TPU v7x, 128 devices: a whole 4x4x4 slice. The times are simulated.
128 devices in a mesh: clip: 16 (over z_hi, y, core), frame: 8 (over x, z_lo).
Axes of the slice: x: 4, y: 4, z: 4 (z_hi: 2, z_lo: 2; z = z_hi * 2 + z_lo), core: 2. Of those that a mesh axis runs over, the one named last changes fastest.
Arguments:
- latents: bfloat16 [128, 784, 640], P(('clip', 'frame')), may hold values from -6 to 6
- timestep: int32 [128], P(('clip', 'frame')), may hold values from 0 to 999
- ref_features: bfloat16 [784, 640], P('clip'), may hold values from -6 to 6
- norm_gains: float32 [3, 640], replicated, may hold values from 0.5 to 1.5
- w_spatial: bfloat16 [4, 640, 640], replicated, as said below
- w_temporal: bfloat16 [4, 640, 640], replicated, as said below
- w_time: bfloat16 [640, 1280], replicated, may hold values from -0.25 to 0.25
- w_in: bfloat16 [640, 5120], replicated, may hold values from -0.25 to 0.25
- w_out: bfloat16 [2560, 640], replicated, may hold values from -0.125 to 0.125
Outputs:
- result: bfloat16 [128, 784, 640], P(('clip', 'frame'))
Inputs may be any that keep to these rules, and one draw needn't show every extreme that they name: `w_spatial`: query, key, value and output projections, in that order. `w_temporal`: query, key, value and output projections, in that order.
All inputs are finite; a program needn't handle non-finite values.
Results may differ from a plain program's by a relative error of at most 0.02.
Values may be sent and summed in bfloat16 or wider, within the bound.
A program may use at most 128 MiB of HBM per device.

v0:
```python
import math

import jax
import jax.numpy as jnp
from jax import lax
from jax.experimental import pallas as pl
from jax.experimental.pallas import tpu as pltpu
from jax.sharding import PartitionSpec as P

HEADS = 8
HEAD = 80
D = 640
FFH = 2560
ROWS = 784
PAD = 128
WIDE = HEADS * PAD
CLIP = 16
FRAME = 8
OWNERS = 7
BLOCK = 112
REF = 49
REF_PAD = 64
KEYS_SELF = 768
KEYS_REF = CLIP * REF_PAD
HALVES = ((0, 64, 0), (448, 48, 64))
LOG2E = 1.4426950408889634
FACTOR = LOG2E / math.sqrt(HEAD)
F32 = jnp.float32
BF16 = jnp.bfloat16
MESH = pl.DeviceIdType.MESH


def dot(a, b):
    return jnp.dot(a, b, preferred_element_type=F32)


def norm(wide):
    mean = jnp.mean(wide, axis=-1, keepdims=True)
    centered = wide - mean
    variance = jnp.mean(centered * centered, axis=-1, keepdims=True)
    return centered * lax.rsqrt(variance + 1e-05)


def iota(shape, axis):
    return lax.broadcasted_iota(jnp.int32, shape, axis)


def head_of(column):
    return (column * 52429) >> 22


def attend(rows, size, keys, q, k_t, v, held, floor, finish, per):
    def columns(n):
        return pl.ds(pl.multiple_of(n * PAD, PAD), PAD)

    def scores(n, slot):
        c = columns(n)
        s = dot(q[rows, c], k_t[c, :])
        held[slot, 0:size, 0:keys] = s
        top = jnp.max(s, axis=1, keepdims=True)
        return top if floor is None else jnp.maximum(top, floor(c))

    @pl.loop(0, HEADS // per)
    def _(i):
        top = scores(i * per, 0)
        for n in range(per):
            c = columns(i * per + n)
            later = scores(i * per + n + 1, (n + 1) % 2) if n + 1 < per else None
            weights = jnp.exp2(held[n % 2, 0:size, 0:keys] - top).astype(BF16)
            finish(c, top, dot(weights, v[:, c]))
            top = later


def body(
    lat, ref, emb, gains, w_spatial, w_temporal, w_time, w_in, w_out, out,
    x, first, h, q, k_t, v, ref_stage, ref_all, kr_t, vr, acc, held, attn, wq, wk, wv, wo,
    ws, wt, wtime, win, wout, mod, spread, gather,
    recv_a, recv_b, moved_a, moved_b, ret, inner,
    sem_x, sem_w, sem_out, ref_send, ref_recv, go_send, go_recv, back_send, back_recv,
):
    swap = ws.at[0]
    wtp = (ws.at[1], ws.at[2], ws.at[3], wt.at[0])
    tq, tk, tv, mixed = (w.at[0:512, 0:D] for w in (wq, wk, wv, wtime))
    result = ret

    me_c = lax.axis_index("clip")
    me_f = lax.axis_index("frame")

    loads_x = []
    for half, (start, count, inside) in enumerate(HALVES):
        for j in range(OWNERS):
            loads_x.append(
                pltpu.make_async_copy(
                    lat.at[pl.ds(BLOCK * j + inside, count)],
                    x.at[pl.ds(start + count * j, count)],
                    sem_x.at[half * OWNERS + j],
                )
            )
    loads_ws = [pltpu.make_async_copy(w_spatial.at[i], ws.at[i], sem_w.at[4 + i]) for i in range(4)]
    load_wtime = pltpu.make_async_copy(w_time, wtime, sem_w.at[0])
    load_wt = pltpu.make_async_copy(w_temporal, wt, sem_w.at[1])
    load_win = pltpu.make_async_copy(w_in, win, sem_w.at[2])
    load_wout = pltpu.make_async_copy(w_out, wout, sem_w.at[3])
    for load in loads_x:
        load.start()
    for load in loads_ws:
        load.start()

    ref_stage[...] = jnp.zeros_like(ref_stage)
    ref_stage[0:REF, :] = ref[...]

    z_hi, y, core = lax.div(me_c, 8), lax.rem(lax.div(me_c, 2), 4), lax.rem(me_c, 2)
    other_frame = me_f + 1 - 2 * lax.rem(me_f, 2)
    sibling = me_c + 1 - 2 * core
    routes = [(0, dy) for dy in (1, 2, 3)] + [(1, dy) for dy in range(4)]

    def clip_of(far, dy, at_core):
        half = (1 - z_hi) if far else z_hi
        return half * 8 + lax.rem(y + dy, 4) * 2 + at_core

    targets = [(clip_of(far, dy, core), other_frame if far else me_f) for far, dy in routes]
    targets.append((sibling, me_f))
    barrier = pltpu.get_barrier_semaphore()
    for clip, frame in targets:
        pl.semaphore_signal(
            barrier, inc=1, device_id={"clip": clip, "frame": frame}, device_id_type=MESH
        )

    @pl.loop(1, FRAME)
    def _(d):
        pl.semaphore_signal(
            barrier,
            inc=1,
            device_id={"clip": me_c, "frame": lax.rem(me_f + d, FRAME)},
            device_id_type=MESH,
        )

    pl.semaphore_wait(barrier, len(targets) + FRAME - 1)

    def ref_rows(clip):
        return ref_all.at[pl.ds(pl.multiple_of(clip * REF_PAD, REF_PAD), REF_PAD)]

    def ref_copy(slot):
        clip, frame = targets[slot]
        return pltpu.make_async_remote_copy(
            src_ref=ref_stage,
            dst_ref=ref_rows(me_c),
            send_sem=ref_send.at[slot],
            recv_sem=ref_recv.at[slot],
            device_id={"clip": clip, "frame": frame},
            device_id_type=MESH,
        )

    def ref_forward(slot):
        far, dy = routes[slot]
        piece = ref_rows(clip_of(far, 4 - dy, core))
        return pltpu.make_async_remote_copy(
            src_ref=piece,
            dst_ref=piece,
            send_sem=ref_send.at[8 + slot],
            recv_sem=ref_recv.at[8 + slot],
            device_id={"clip": sibling, "frame": me_f},
            device_id_type=MESH,
        )

    for slot in range(8):
        ref_copy(slot).start()

    ref_all[pl.ds(pl.multiple_of(me_c * REF_PAD, REF_PAD), REF_PAD), :] = ref_stage[...]

    wq[...] = jnp.zeros_like(wq)
    wk[...] = jnp.zeros_like(wk)
    wv[...] = jnp.zeros_like(wv)
    wo[...] = jnp.zeros_like(wo)

    for load in loads_x:
        load.wait()

    @pl.loop(0, ROWS // BLOCK)
    def _(i):
        rows = pl.ds(pl.multiple_of(i * BLOCK, BLOCK), BLOCK)
        h[rows, :] = (norm(x[rows, :].astype(F32)) * gains[0:1, :]).astype(BF16)

    for i, target in enumerate((wq, wk, wv)):
        loads_ws[i].wait()
        for n in range(HEADS):
            target[:, PAD * n : PAD * n + HEAD] = ws[i, :, HEAD * n : HEAD * n + HEAD]
    loads_ws[3].wait()
    for n in range(HEADS):
        wo[PAD * n : PAD * n + HEAD, :] = ws[3, HEAD * n : HEAD * n + HEAD, :]
    load_wtime.start()
    load_wt.start()
    load_win.start()
    load_wout.start()

    for j in range(WIDE // 256):
        c = pl.ds(j * 256, 256)
        lane = iota((1, 256), 1) & (PAD - 1)
        q[:, c] = jnp.where(lane == HEAD, 1.0, dot(h[...], wq[:, c]) * FACTOR).astype(BF16)
        k_t[c, :] = dot(h[0:KEYS_SELF, :], wk[:, c]).astype(BF16).T
        v[:, c] = jnp.where(lane == HEAD, 1.0, dot(h[0:KEYS_SELF, :], wv[:, c])).astype(BF16)

    def own(c, top, o):
        acc[:, c] = jnp.where(iota((1, PAD), 1) == HEAD + 1, top, o)

    attend(pl.ds(0, ROWS), ROWS, KEYS_SELF, q, k_t, v, held, None, own, 4)

    for slot in range(7):
        ref_copy(slot).wait_recv()
        ref_forward(slot).start()
    load_wtime.wait()
    mod[...] = dot(jnp.broadcast_to(emb[...], (16, D)), wtime[...])

    load_wt.wait()
    column = iota((D, D), 1)
    source = HEAD * ((column & (PAD - 1)) >> 4) + 16 * (column >> 7) + (column & 15)
    swap[...] = (iota((D, D), 0) == source).astype(F32).astype(BF16)
    for i in range(3):
        for c0, c1 in ((0, 256), (256, 512), (512, D)):
            wtp[i][:, c0:c1] = dot(wt[i], swap[:, c0:c1]).astype(BF16)
    for n in range(HEADS):
        for r in range(D // PAD):
            wtp[3][PAD * r + 16 * n : PAD * r + 16 * n + 16, :] = wt[
                3, HEAD * n + 16 * r : HEAD * n + 16 * r + 16, :
            ]
    place = iota((FRAME * PAD, PAD), 0)
    pair = FRAME * (place >> 7) + ((place & (PAD - 1)) >> 4)
    gather[...] = ((iota((FRAME * PAD, PAD), 1) & 63) == pair).astype(F32).astype(BF16)
    place = iota((PAD, FRAME * PAD), 1)
    pair = FRAME * (place >> 7) + ((place & (PAD - 1)) >> 4)
    spread[...] = (iota((PAD, FRAME * PAD), 0) == pair).astype(F32).astype(BF16)

    ref_copy(7).wait_recv()
    for slot in range(7):
        ref_forward(slot).wait()

    row = iota((PAD, 16), 0)
    tail = iota((PAD, 16), 1)
    place = ((row < REF_PAD) & (row == tail + REF)) | ((row == REF_PAD + REF) & (tail == 15))
    placed = dot(place.astype(F32).astype(BF16), h[KEYS_SELF:ROWS, :])
    ref_all[0:PAD, :] = (ref_all[0:PAD, :].astype(F32) + placed).astype(BF16)

    for j in range(WIDE // 256):
        c = pl.ds(j * 256, 256)
        lane = iota((1, 256), 1) & (PAD - 1)
        key = iota((KEYS_REF, 1), 0)
        valid = ((key & (REF_PAD - 1)) < REF) | (key < REF_PAD) | (key == REF_PAD + REF)
        mask = jnp.where(valid, 0.0, -1e30)
        kr_t[c, :] = jnp.where(lane == HEAD, mask, dot(ref_all[...], wk[:, c])).astype(BF16).T
        vr[:, c] = jnp.where(lane == HEAD, 1.0, dot(ref_all[...], wv[:, c])).astype(BF16)

    def go_copy(half, d):
        start, count, _ = HALVES[half]
        target = lax.rem(me_f + d, FRAME)
        block = lax.min(target, OWNERS - 1)
        return pltpu.make_async_remote_copy(
            src_ref=h.at[pl.ds(pl.multiple_of(start + block * count, 16), count)],
            dst_ref=(recv_a, recv_b)[half].at[me_f],
            send_sem=go_send.at[half * FRAME + d],
            recv_sem=go_recv.at[half * FRAME + d],
            device_id={"clip": me_c, "frame": target},
            device_id_type=MESH,
        )

    def is_owner(d):
        return lax.rem(me_f + d, FRAME) < OWNERS

    def comes_from_owner(d):
        return lax.rem(me_f + FRAME - d, FRAME) < OWNERS

    for half, (start, count, _) in enumerate(HALVES):
        size = count * OWNERS
        rows = pl.ds(start, size)

        def own_top(c):
            return acc[rows, c][:, HEAD + 1 : HEAD + 2]

        def merge(c, top, o):
            before = acc[rows, c]
            o = o + before * jnp.exp2(before[:, HEAD + 1 : HEAD + 2] - top)
            attn[0:size, c] = (o * (1.0 / o[:, HEAD : HEAD + 1])).astype(BF16)

        attend(rows, size, KEYS_REF, q, kr_t, vr, held, own_top, merge, 4)

        for c0, c1 in ((0, 256), (256, 512), (512, D)):
            first[rows, c0:c1] = (
                x[rows, c0:c1].astype(F32) + dot(attn[0:size, :], wo[:, c0:c1])
            ).astype(BF16)

        @pl.loop(0, OWNERS)
        def _(i):
            part = pl.ds(pl.multiple_of(start + i * count, 16), count)
            normed = norm(first[part, :].astype(F32)) * gains[1:2, :]
            h[part, :] = (normed * (1.0 + mod[0:1, D:]) + mod[0:1, :D]).astype(BF16)

        @pl.loop(1, FRAME)
        def _(d):
            @pl.when(is_owner(d))
            def _():
                go_copy(half, d).start()

        @pl.when(me_f < OWNERS)
        def _():
            (recv_a, recv_b)[half][me_f] = h[
                pl.ds(pl.multiple_of(start + lax.min(me_f, OWNERS - 1) * count, 16), count), :
            ]

    def back_copy(half, d):
        start, count, _ = HALVES[half]
        target = lax.rem(me_f + d, FRAME)
        return pltpu.make_async_remote_copy(
            src_ref=(moved_a, moved_b)[half].at[target],
            dst_ref=ret.at[pl.ds(pl.multiple_of(start + lax.min(me_f, OWNERS - 1) * count, 16), count)],
            send_sem=back_send.at[half * FRAME + d],
            recv_sem=back_recv.at[half * FRAME + d],
            device_id={"clip": me_c, "frame": target},
            device_id_type=MESH,
        )

    @pl.when(me_f < OWNERS)
    def _():
        for half, (start, count, _) in enumerate(HALVES):
            size = count * FRAME
            recv = (recv_a, recv_b)[half]
            moved = (moved_a, moved_b)[half]

            @pl.loop(1, FRAME)
            def _(d):
                go_copy(half, d).wait_recv()

            for c0, c1 in ((0, 256), (256, 512), (512, D)):
                states = recv[...].reshape(size, D)
                tq[0:size, c0:c1] = (dot(states, wtp[0][:, c0:c1]) * FACTOR).astype(BF16)
                tk[0:size, c0:c1] = dot(states, wtp[1][:, c0:c1]).astype(BF16)
                tv[0:size, c0:c1] = dot(states, wtp[2][:, c0:c1]).astype(BF16)

            @pl.loop(0, FRAME)
            def _(f):
                own_rows = pl.ds(pl.multiple_of(f * count, 16), count)
                queries = tq[own_rows, :].astype(F32)
                for g in range(FRAME):
                    pairs = queries * tk[g * count : (g + 1) * count, :].astype(F32)
                    part = pairs[:, 0:PAD]
                    for r in range(1, D // PAD):
                        part = part + pairs[:, PAD * r : PAD * r + PAD]
                    attn[own_rows, PAD * g : PAD * g + PAD] = part.astype(BF16)

            s = dot(attn[0:size, :], gather[...])
            top = s
            for shift in (8, 16, 32):
                top = jnp.maximum(top, pltpu.roll(top, shift, 1))
            e = jnp.exp2(s - top)
            total = e
            for shift in (8, 16, 32):
                total = total + pltpu.roll(total, shift, 1)
            weights = (e / total).astype(BF16)
            for c0 in range(0, FRAME * PAD, 256):
                held[0, 0:size, c0 : c0 + 256] = dot(weights, spread[:, c0 : c0 + 256])
            @pl.loop(0, FRAME)
            def _(f):
                own_rows = pl.ds(pl.multiple_of(f * count, 16), count)
                for r in range(D // PAD):
                    c = slice(PAD * r, PAD * r + PAD)
                    sums = None
                    for g in range(FRAME):
                        term = held[0, own_rows, PAD * g : PAD * g + PAD] * tv[
                            g * count : (g + 1) * count, c
                        ].astype(F32)
                        sums = term if sums is None else sums + term
                    mixed[own_rows, c] = sums.astype(BF16)

            for c0, c1 in ((0, 256), (256, 512), (512, D)):
                moved[:, :, c0:c1] = (
                    dot(mixed[0:size, :], wtp[3][:, c0:c1]).astype(BF16).reshape(FRAME, count, c1 - c0)
                )

            @pl.loop(1, FRAME)
            def _(d):
                back_copy(half, d).start()

            ret[pl.ds(pl.multiple_of(start + lax.min(me_f, OWNERS - 1) * count, 16), count), :] = moved[
                me_f
            ]

    load_win.wait()
    load_wout.wait()
    stores = []
    for half, (start, count, inside) in enumerate(HALVES):
        size = count * OWNERS
        rows = pl.ds(start, size)

        @pl.loop(1, FRAME)
        def _(d):
            @pl.when(comes_from_owner(d))
            def _():
                back_copy(half, d).wait_recv()

        @pl.loop(0, OWNERS)
        def _(i):
            part = pl.ds(pl.multiple_of(start + i * count, 16), count)
            second = (first[part, :].astype(F32) + ret[part, :].astype(F32)).astype(BF16)
            x[part, :] = second
            first[part, :] = (norm(second.astype(F32)) * gains[2:3, :]).astype(BF16)

        @pl.loop(0, 2)
        def _(i):
            for j in range(FFH // 512):
                c = pl.ds(pl.multiple_of(i * (FFH // 2) + 256 * j, 256), 256)
                g = pl.ds(pl.multiple_of(FFH + i * (FFH // 2) + 256 * j, 256), 256)
                value = dot(first[rows, :], win[:, c])
                gate = dot(first[rows, :], win[:, g])
                gelu = 0.5 * gate * (1.0 + lax.erf(gate * (1.0 / math.sqrt(2.0))))
                inner[0:size, c] = (value * gelu).astype(BF16)

        for c0, c1 in ((0, 256), (256, 512), (512, D)):
            result[rows, c0:c1] = (
                x[rows, c0:c1].astype(F32) + dot(inner[0:size, :], wout[:, c0:c1])
            ).astype(BF16)
        for j in range(OWNERS):
            store = pltpu.make_async_copy(
                result.at[pl.ds(start + count * j, count)],
                out.at[pl.ds(BLOCK * j + inside, count)],
                sem_out.at[half * OWNERS + j],
            )
            store.start()
            stores.append(store)

    for slot in range(8):
        ref_copy(slot).wait_send()

    for half in range(2):

        @pl.loop(1, FRAME)
        def _(d):
            @pl.when(is_owner(d))
            def _():
                go_copy(half, d).wait_send()

            @pl.when(me_f < OWNERS)
            def _():
                back_copy(half, d).wait_send()

    for store in stores:
        store.wait()


def time_embedding(steps):
    half = D // 2
    freqs = jnp.exp(-math.log(10000.0) * jnp.arange(half, dtype=F32) / half)
    angles = steps.astype(F32)[:, None] * freqs[None, :]
    return jnp.concatenate([jnp.cos(angles), jnp.sin(angles)], axis=-1).astype(BF16)


def per_device(
    latents, timestep, ref_features, norm_gains, w_spatial, w_temporal, w_time, w_in, w_out
):
    emb = time_embedding(timestep)
    vmem = pl.BlockSpec(memory_space=pltpu.VMEM)
    hbm = pl.BlockSpec(memory_space=pl.ANY)
    sems = pltpu.SemaphoreType.DMA
    result = pl.pallas_call(
        body,
        out_shape=jax.ShapeDtypeStruct((ROWS, D), BF16),
        in_specs=[hbm, vmem, vmem, vmem, hbm, hbm, hbm, hbm, hbm],
        out_specs=hbm,
        scratch_shapes=[
            pltpu.VMEM((ROWS, D), BF16),
            pltpu.VMEM((ROWS, D), BF16),
            pltpu.VMEM((ROWS, D), BF16),
            pltpu.VMEM((ROWS, WIDE), BF16),
            pltpu.VMEM((WIDE, KEYS_SELF), BF16),
            pltpu.VMEM((KEYS_SELF, WIDE), BF16),
            pltpu.VMEM((REF_PAD, D), BF16),
            pltpu.VMEM((KEYS_REF, D), BF16),
            pltpu.VMEM((WIDE, KEYS_REF), BF16),
            pltpu.VMEM((KEYS_REF, WIDE), BF16),
            pltpu.VMEM((ROWS, WIDE), F32),
            pltpu.VMEM((2, ROWS, KEYS_REF), F32),
            pltpu.VMEM((512, WIDE), BF16),
            pltpu.VMEM((D, WIDE), BF16),
            pltpu.VMEM((D, WIDE), BF16),
            pltpu.VMEM((D, WIDE), BF16),
            pltpu.VMEM((WIDE, D), BF16),
            pltpu.VMEM((4, D, D), BF16),
            pltpu.VMEM((4, D, D), BF16),
            pltpu.VMEM((D, 2 * D), BF16),
            pltpu.VMEM((D, 2 * FFH), BF16),
            pltpu.VMEM((FFH, D), BF16),
            pltpu.VMEM((16, 2 * D), F32),
            pltpu.VMEM((PAD, FRAME * PAD), BF16),
            pltpu.VMEM((FRAME * PAD, PAD), BF16),
            pltpu.VMEM((FRAME, 64, D), BF16),
            pltpu.VMEM((FRAME, 48, D), BF16),
            pltpu.VMEM((FRAME, 64, D), BF16),
            pltpu.VMEM((FRAME, 48, D), BF16),
            pltpu.VMEM((ROWS, D), BF16),
            pltpu.VMEM((448, FFH), BF16),
            sems((2 * OWNERS,)),
            sems((8,)),
            sems((2 * OWNERS,)),
            sems((CLIP,)),
            sems((CLIP,)),
            sems((2 * FRAME,)),
            sems((2 * FRAME,)),
            sems((2 * FRAME,)),
            sems((2 * FRAME,)),
        ],
        compiler_params=pltpu.CompilerParams(
            collective_id=0, has_side_effects=True, vmem_limit_bytes=60 * 1024 * 1024
        ),
        name="block",
    )(latents[0], ref_features, emb, norm_gains, w_spatial, w_temporal, w_time, w_in, w_out)
    return result[None]


def solution(mesh):
    placed = (
        P(("clip", "frame"), None, None),
        P(("clip", "frame")),
        P("clip", None),
        P(),
        P(),
        P(),
        P(),
        P(),
        P(),
    )
    return jax.shard_map(
        per_device,
        mesh=mesh,
        in_specs=placed,
        out_specs=P(("clip", "frame"), None, None),
        check_vma=False,
    )
```

profile of v0, /device:TPU:32, one launch (start us, length us, event | category | flops | bytes accessed | tf_op | source)
XLA Modules:
  0.0 83.6 jit_solution(12557100346196602387)
XLA Ops:
  0.7 0.1 sine_convert_fusion
  0.7 0.7 pad_maximum_fusion.emb
  1.4 80.0 %block.1 = bf16[784,640]{1,0:T(8,128)(2,1)} custom-call(bf16[784,640]{1,0:T(8,128)(2,1)} %bitcast.4, bf16[49,640]{1,0:T(8,128)(2,1)} %ref.1, bf16[1,640]{1,0:T(2,128)(2,1)} %pad_maximum_fusion.emb, f32[3,640]{1,0:T(4,128)} %gains.1, bf16[4,640,640]{2,1,0:T(8,128)(2,1)} %w_spatial.1, bf16[4,640,640]{2,1,0:T(8,128)(2,1)} %w_temporal.1, ...), custom_call_target="tpu_custom_call" | custom-call | tf_op jit(solution)/shard_map/block/pallas_call | solution.py:461
  81.4 2.2 %copy.12 = bf16[1,784,640]{2,1,0:T(8,128)(2,1)} copy(bf16[1,784,640]{2,1,0:T(8,128)(2,1)} %bitcast.3) | data formatting | bytes 2007040
  (2 shorter events, 0.0 us)
where the time goes:
time: 83.8 us; the launch traced here: 83.6 us
  Pallas kernels  80 us (95%)
  local copies, waits for them, and re-layouts  2.26 us (3%)
    pallas_call x1, Pallas kernels, per_device(): pl.pallas_call(body, out_shape=jax.ShapeDtypeStruct((ROWS, D), BF16), in_...  80 us
    unnamed x1, local copies, waits for them, and re-layouts  2.25 us

commit v1 on v0

--- a/solution.py
+++ b/solution.py
@@ -81,7 +81,7 @@
     swap = ws.at[0]
     wtp = (ws.at[1], ws.at[2], ws.at[3], wt.at[0])
     tq, tk, tv, mixed = (w.at[0:512, 0:D] for w in (wq, wk, wv, wtime))
-    result = ret
+    result = acc.at[:, 0:D]
 
     me_c = lax.axis_index("clip")
     me_f = lax.axis_index("frame")
@@ -280,7 +280,7 @@
             o = o + before * jnp.exp2(before[:, HEAD + 1 : HEAD + 2] - top)
             attn[0:size, c] = (o * (1.0 / o[:, HEAD : HEAD + 1])).astype(BF16)
 
-        attend(rows, size, KEYS_REF, q, kr_t, vr, held, own_top, merge, 4)
+        attend(rows, size, KEYS_REF, q, kr_t, vr, held, own_top, merge, 8)
 
         for c0, c1 in ((0, 256), (256, 512), (512, D)):
             first[rows, c0:c1] = (
@@ -334,16 +334,19 @@
                 tk[0:size, c0:c1] = dot(states, wtp[1][:, c0:c1]).astype(BF16)
                 tv[0:size, c0:c1] = dot(states, wtp[2][:, c0:c1]).astype(BF16)
 
-            @pl.loop(0, FRAME)
-            def _(f):
-                own_rows = pl.ds(pl.multiple_of(f * count, 16), count)
-                queries = tq[own_rows, :].astype(F32)
-                for g in range(FRAME):
-                    pairs = queries * tk[g * count : (g + 1) * count, :].astype(F32)
-                    part = pairs[:, 0:PAD]
-                    for r in range(1, D // PAD):
-                        part = part + pairs[:, PAD * r : PAD * r + PAD]
-                    attn[own_rows, PAD * g : PAD * g + PAD] = part.astype(BF16)
+            def at(f, i):
+                return pl.ds(pl.multiple_of(f * count + 16 * i, 16), 16)
+
+            @pl.loop(0, count // 16)
+            def _(i):
+                for f in range(FRAME):
+                    queries = tq[at(f, i), :]
+                    for g in range(FRAME):
+                        pairs = queries * tk[at(g, i), :]
+                        part = pairs[:, 0:PAD]
+                        for r in range(1, D // PAD):
+                            part = part + pairs[:, PAD * r : PAD * r + PAD]
+                        attn[at(f, i), PAD * g : PAD * g + PAD] = part
 
             s = dot(attn[0:size, :], gather[...])
             top = s
@@ -355,19 +358,20 @@
                 total = total + pltpu.roll(total, shift, 1)
             weights = (e / total).astype(BF16)
             for c0 in range(0, FRAME * PAD, 256):
-                held[0, 0:size, c0 : c0 + 256] = dot(weights, spread[:, c0 : c0 + 256])
-            @pl.loop(0, FRAME)
-            def _(f):
-                own_rows = pl.ds(pl.multiple_of(f * count, 16), count)
-                for r in range(D // PAD):
-                    c = slice(PAD * r, PAD * r + PAD)
-                    sums = None
-                    for g in range(FRAME):
-                        term = held[0, own_rows, PAD * g : PAD * g + PAD] * tv[
-                            g * count : (g + 1) * count, c
-                        ].astype(F32)
-                        sums = term if sums is None else sums + term
-                    mixed[own_rows, c] = sums.astype(BF16)
+                attn[0:size, c0 : c0 + 256] = dot(weights, spread[:, c0 : c0 + 256]).astype(BF16)
+
+            @pl.loop(0, count // 16)
+            def _(i):
+                for f in range(FRAME):
+                    for r in range(D // PAD):
+                        c = slice(PAD * r, PAD * r + PAD)
+                        terms = [
+                            attn[at(f, i), PAD * g : PAD * g + PAD] * tv[at(g, i), c]
+                            for g in range(FRAME)
+                        ]
+                        while len(terms) > 1:
+                            terms = [a + b for a, b in zip(terms[0::2], terms[1::2])]
+                        mixed[at(f, i), c] = terms[0]
 
             for c0, c1 in ((0, 256), (256, 512), (512, D)):
                 moved[:, :, c0:c1] = (
@@ -413,9 +417,9 @@
                 inner[0:size, c] = (value * gelu).astype(BF16)
 
         for c0, c1 in ((0, 256), (256, 512), (512, D)):
-            result[rows, c0:c1] = (
-                x[rows, c0:c1].astype(F32) + dot(inner[0:size, :], wout[:, c0:c1])
-            ).astype(BF16)
+            result[rows, c0:c1] = x[rows, c0:c1].astype(F32) + dot(
+                inner[0:size, :], wout[:, c0:c1]
+            )
         for j in range(OWNERS):
             store = pltpu.make_async_copy(
                 result.at[pl.ds(start + count * j, count)],
@@ -460,7 +464,7 @@
     sems = pltpu.SemaphoreType.DMA
     result = pl.pallas_call(
         body,
-        out_shape=jax.ShapeDtypeStruct((ROWS, D), BF16),
+        out_shape=jax.ShapeDtypeStruct((ROWS, D), F32),
         in_specs=[hbm, vmem, vmem, vmem, hbm, hbm, hbm, hbm, hbm],
         out_specs=hbm,
         scratch_shapes=[
@@ -510,7 +514,7 @@
         ),
         name="block",
     )(latents[0], ref_features, emb, norm_gains, w_spatial, w_temporal, w_time, w_in, w_out)
-    return result[None]
+    return result.astype(BF16)[None]
 
 
 def solution(mesh):

time: 83.8 us -> 84.2 us (level)
  other arithmetic: 0.7 us -> 3.32 us
  local copies, waits for them, and re-layouts: 2.26 us -> 0.01 us
    broadcast_in_dim x0 -> x1, other arithmetic: none -> 2.62 us  [per_device(): return result.astype(BF16)[None]]
    unnamed x1 -> x0, local copies, waits for them, and re-layouts: 2.25 us -> none
where the time goes in v1:
time: 84.2 us; the launch traced here: 84 us
  Pallas kernels  80 us (95%)
  other arithmetic  3.32 us (4%)
    pallas_call x1, Pallas kernels, per_device(): pl.pallas_call(body, out_shape=jax.ShapeDtypeStruct((ROWS, D), F32), in_s...  80 us
    broadcast_in_dim x1, other arithmetic, per_device(): return result.astype(BF16)[None]  2.62 us

profile of v1, /device:TPU:32, one launch (start us, length us, event | category | flops | bytes accessed | tf_op | source)
XLA Modules:
  0.0 84.0 jit_solution(16383972012642159652)
XLA Ops:
  0.7 0.1 sine_convert_fusion
  0.7 0.7 pad_maximum_fusion.emb
  1.4 80.0 %block.1 = f32[784,640]{1,0:T(8,128)} custom-call(bf16[784,640]{1,0:T(8,128)(2,1)} %bitcast.4, bf16[49,640]{1,0:T(8,128)(2,1)} %ref.1, bf16[1,640]{1,0:T(2,128)(2,1)} %pad_maximum_fusion.emb, f32[3,640]{1,0:T(4,128)} %gains.1, bf16[4,640,640]{2,1,0:T(8,128)(2,1)} %w_spatial.1, bf16[4,640,640]{2,1,0:T(8,128)(2,1)} %w_temporal.1, bf16[640,1280]{1,0:T(8,128)(2,1)} %w_time.1, ...), custom_call_target="tpu_custom_call" | custom-call | tf_op jit(solution)/shard_map/block/pallas_call | solution.py:465
  81.3 2.6 %convert_bitcast_fusion = bf16[1,784,640]{2,1,0:T(8,128)(2,1)} fusion(f32[784,640]{1,0:T(8,128)} %block.1), kind=kLoop, calls=%fused_computation | loop fusion | flops 501760 | bytes 3010560 | tf_op jit(solution)/shard_map/broadcast_in_dim | solution.py:517
  (2 shorter events, 0.0 us)

commit v2 on v1

--- a/solution.py
+++ b/solution.py
@@ -81,7 +81,7 @@
     swap = ws.at[0]
     wtp = (ws.at[1], ws.at[2], ws.at[3], wt.at[0])
     tq, tk, tv, mixed = (w.at[0:512, 0:D] for w in (wq, wk, wv, wtime))
-    result = acc.at[:, 0:D]
+    result = ret
 
     me_c = lax.axis_index("clip")
     me_f = lax.axis_index("frame")
@@ -200,16 +200,112 @@
         k_t[c, :] = dot(h[0:KEYS_SELF, :], wk[:, c]).astype(BF16).T
         v[:, c] = jnp.where(lane == HEAD, 1.0, dot(h[0:KEYS_SELF, :], wv[:, c])).astype(BF16)
 
-    def own(c, top, o):
-        acc[:, c] = jnp.where(iota((1, PAD), 1) == HEAD + 1, top, o)
-
-    attend(pl.ds(0, ROWS), ROWS, KEYS_SELF, q, k_t, v, held, None, own, 4)
+    def attend_own(half):
+        start, count, _ = HALVES[half]
+        rows = pl.ds(start, count * OWNERS)
+
+        def own(c, top, o):
+            acc[rows, c] = jnp.where(iota((1, PAD), 1) == HEAD + 1, top, o)
+
+        attend(rows, count * OWNERS, KEYS_SELF, q, k_t, v, held, None, own, 4)
 
     for slot in range(7):
         ref_copy(slot).wait_recv()
         ref_forward(slot).start()
+    attend_own(0)
+
     load_wtime.wait()
     mod[...] = dot(jnp.broadcast_to(emb[...], (16, D)), wtime[...])
+
+    ref_copy(7).wait_recv()
+    for slot in range(7):
+        ref_forward(slot).wait()
+
+    row = iota((PAD, 16), 0)
+    tail = iota((PAD, 16), 1)
+    place = ((row < REF_PAD) & (row == tail + REF)) | ((row == REF_PAD + REF) & (tail == 15))
+    placed = dot(place.astype(F32).astype(BF16), h[KEYS_SELF:ROWS, :])
+    ref_all[0:PAD, :] = (ref_all[0:PAD, :].astype(F32) + placed).astype(BF16)
+
+    for j in range(WIDE // 256):
+        c = pl.ds(j * 256, 256)
+        lane = iota((1, 256), 1) & (PAD - 1)
+        key = iota((KEYS_REF, 1), 0)
+        valid = ((key & (REF_PAD - 1)) < REF) | (key < REF_PAD) | (key == REF_PAD + REF)
+        mask = jnp.where(valid, 0.0, -1e30)
+        kr_t[c, :] = jnp.where(lane == HEAD, mask, dot(ref_all[...], wk[:, c])).astype(BF16).T
+        vr[:, c] = jnp.where(lane == HEAD, 1.0, dot(ref_all[...], wv[:, c])).astype(BF16)
+
+    def go_copy(half, d):
+        start, count, _ = HALVES[half]
+        target = lax.rem(me_f + d, FRAME)
+        block = lax.min(target, OWNERS - 1)
+        return pltpu.make_async_remote_copy(
+            src_ref=h.at[pl.ds(pl.multiple_of(start + block * count, 16), count)],
+            dst_ref=(recv_a, recv_b)[half].at[me_f],
+            send_sem=go_send.at[half * FRAME + d],
+            recv_sem=go_recv.at[half * FRAME + d],
+            device_id={"clip": me_c, "frame": target},
+            device_id_type=MESH,
+        )
+
+    def is_owner(d):
+        return lax.rem(me_f + d, FRAME) < OWNERS
+
+    def comes_from_owner(d):
+        return lax.rem(me_f + FRAME - d, FRAME) < OWNERS
+
+    for half, (start, count, _) in enumerate(HALVES):
+        size = count * OWNERS
+        rows = pl.ds(start, size)
+
+        if half == 1:
+            attend_own(1)
+
+        def own_top(c):
+            return acc[rows, c][:, HEAD + 1 : HEAD + 2]
+
+        def merge(c, top, o):
+            before = acc[rows, c]
+            o = o + before * jnp.exp2(before[:, HEAD + 1 : HEAD + 2] - top)
+            attn[0:size, c] = (o * (1.0 / o[:, HEAD : HEAD + 1])).astype(BF16)
+
+        attend(rows, size, KEYS_REF, q, kr_t, vr, held, own_top, merge, 8)
+
+        for c0, c1 in ((0, 256), (256, 512), (512, D)):
+            first[rows, c0:c1] = (
+                x[rows, c0:c1].astype(F32) + dot(attn[0:size, :], wo[:, c0:c1])
+            ).astype(BF16)
+
+        @pl.loop(0, OWNERS)
+        def _(i):
+            part = pl.ds(pl.multiple_of(start + i * count, 16), count)
+            normed = norm(first[part, :].astype(F32)) * gains[1:2, :]
+            h[part, :] = (normed * (1.0 + mod[0:1, D:]) + mod[0:1, :D]).astype(BF16)
+
+        @pl.loop(1, FRAME)
+        def _(d):
+            @pl.when(is_owner(d))
+            def _():
+                go_copy(half, d).start()
+
+        @pl.when(me_f < OWNERS)
+        def _():
+            (recv_a, recv_b)[half][me_f] = h[
+                pl.ds(pl.multiple_of(start + lax.min(me_f, OWNERS - 1) * count, 16), count), :
+            ]
+
+    def back_copy(half, d):
+        start, count, _ = HALVES[half]
+        target = lax.rem(me_f + d, FRAME)
+        return pltpu.make_async_remote_copy(
+            src_ref=(moved_a, moved_b)[half].at[target],
+            dst_ref=ret.at[pl.ds(pl.multiple_of(start + lax.min(me_f, OWNERS - 1) * count, 16), count)],
+            send_sem=back_send.at[half * FRAME + d],
+            recv_sem=back_recv.at[half * FRAME + d],
+            device_id={"clip": me_c, "frame": target},
+            device_id_type=MESH,
+        )
 
     load_wt.wait()
     column = iota((D, D), 1)
@@ -230,93 +326,6 @@
     pair = FRAME * (place >> 7) + ((place & (PAD - 1)) >> 4)
     spread[...] = (iota((PAD, FRAME * PAD), 0) == pair).astype(F32).astype(BF16)
 
-    ref_copy(7).wait_recv()
-    for slot in range(7):
-        ref_forward(slot).wait()
-
-    row = iota((PAD, 16), 0)
-    tail = iota((PAD, 16), 1)
-    place = ((row < REF_PAD) & (row == tail + REF)) | ((row == REF_PAD + REF) & (tail == 15))
-    placed = dot(place.astype(F32).astype(BF16), h[KEYS_SELF:ROWS, :])
-    ref_all[0:PAD, :] = (ref_all[0:PAD, :].astype(F32) + placed).astype(BF16)
-
-    for j in range(WIDE // 256):
-        c = pl.ds(j * 256, 256)
-        lane = iota((1, 256), 1) & (PAD - 1)
-        key = iota((KEYS_REF, 1), 0)
-        valid = ((key & (REF_PAD - 1)) < REF) | (key < REF_PAD) | (key == REF_PAD + REF)
-        mask = jnp.where(valid, 0.0, -1e30)
-        kr_t[c, :] = jnp.where(lane == HEAD, mask, dot(ref_all[...], wk[:, c])).astype(BF16).T
-        vr[:, c] = jnp.where(lane == HEAD, 1.0, dot(ref_all[...], wv[:, c])).astype(BF16)
-
-    def go_copy(half, d):
-        start, count, _ = HALVES[half]
-        target = lax.rem(me_f + d, FRAME)
-        block = lax.min(target, OWNERS - 1)
-        return pltpu.make_async_remote_copy(
-            src_ref=h.at[pl.ds(pl.multiple_of(start + block * count, 16), count)],
-            dst_ref=(recv_a, recv_b)[half].at[me_f],
-            send_sem=go_send.at[half * FRAME + d],
-            recv_sem=go_recv.at[half * FRAME + d],
-            device_id={"clip": me_c, "frame": target},
-            device_id_type=MESH,
-        )
-
-    def is_owner(d):
-        return lax.rem(me_f + d, FRAME) < OWNERS
-
-    def comes_from_owner(d):
-        return lax.rem(me_f + FRAME - d, FRAME) < OWNERS
-
-    for half, (start, count, _) in enumerate(HALVES):
-        size = count * OWNERS
-        rows = pl.ds(start, size)
-
-        def own_top(c):
-            return acc[rows, c][:, HEAD + 1 : HEAD + 2]
-
-        def merge(c, top, o):
-            before = acc[rows, c]
-            o = o + before * jnp.exp2(before[:, HEAD + 1 : HEAD + 2] - top)
-            attn[0:size, c] = (o * (1.0 / o[:, HEAD : HEAD + 1])).astype(BF16)
-
-        attend(rows, size, KEYS_REF, q, kr_t, vr, held, own_top, merge, 8)
-
-        for c0, c1 in ((0, 256), (256, 512), (512, D)):
-            first[rows, c0:c1] = (
-                x[rows, c0:c1].astype(F32) + dot(attn[0:size, :], wo[:, c0:c1])
-            ).astype(BF16)
-
-        @pl.loop(0, OWNERS)
-        def _(i):
-            part = pl.ds(pl.multiple_of(start + i * count, 16), count)
-            normed = norm(first[part, :].astype(F32)) * gains[1:2, :]
-            h[part, :] = (normed * (1.0 + mod[0:1, D:]) + mod[0:1, :D]).astype(BF16)
-
-        @pl.loop(1, FRAME)
-        def _(d):
-            @pl.when(is_owner(d))
-            def _():
-                go_copy(half, d).start()
-
-        @pl.when(me_f < OWNERS)
-        def _():
-            (recv_a, recv_b)[half][me_f] = h[
-                pl.ds(pl.multiple_of(start + lax.min(me_f, OWNERS - 1) * count, 16), count), :
-            ]
-
-    def back_copy(half, d):
-        start, count, _ = HALVES[half]
-        target = lax.rem(me_f + d, FRAME)
-        return pltpu.make_async_remote_copy(
-            src_ref=(moved_a, moved_b)[half].at[target],
-            dst_ref=ret.at[pl.ds(pl.multiple_of(start + lax.min(me_f, OWNERS - 1) * count, 16), count)],
-            send_sem=back_send.at[half * FRAME + d],
-            recv_sem=back_recv.at[half * FRAME + d],
-            device_id={"clip": me_c, "frame": target},
-            device_id_type=MESH,
-        )
-
     @pl.when(me_f < OWNERS)
     def _():
         for half, (start, count, _) in enumerate(HALVES):
@@ -417,9 +426,9 @@
                 inner[0:size, c] = (value * gelu).astype(BF16)
 
         for c0, c1 in ((0, 256), (256, 512), (512, D)):
-            result[rows, c0:c1] = x[rows, c0:c1].astype(F32) + dot(
-                inner[0:size, :], wout[:, c0:c1]
-            )
+            result[rows, c0:c1] = (
+                x[rows, c0:c1].astype(F32) + dot(inner[0:size, :], wout[:, c0:c1])
+            ).astype(BF16)
         for j in range(OWNERS):
             store = pltpu.make_async_copy(
                 result.at[pl.ds(start + count * j, count)],
@@ -464,7 +473,7 @@
     sems = pltpu.SemaphoreType.DMA
     result = pl.pallas_call(
         body,
-        out_shape=jax.ShapeDtypeStruct((ROWS, D), F32),
+        out_shape=jax.ShapeDtypeStruct((ROWS, D), BF16),
         in_specs=[hbm, vmem, vmem, vmem, hbm, hbm, hbm, hbm, hbm],
         out_specs=hbm,
         scratch_shapes=[
@@ -514,7 +523,7 @@
         ),
         name="block",
     )(latents[0], ref_features, emb, norm_gains, w_spatial, w_temporal, w_time, w_in, w_out)
-    return result.astype(BF16)[None]
+    return result[None]
 
 
 def solution(mesh):

time: 84.2 us -> 80.5 us (0.956)
  Pallas kernels: 80 us -> 76.6 us
  other arithmetic: 3.32 us -> 0.7 us
  local copies, waits for them, and re-layouts: 0.01 us -> 2.26 us
    pallas_call x1, Pallas kernels: 80 us -> 76.6 us  [per_device(): pl.pallas_call(body, out_shape=jax.ShapeDtypeStruct((ROWS, D), BF16), in_...]
    broadcast_in_dim x1 -> x0, other arithmetic: 2.62 us -> none  [per_device(): return result.astype(BF16)[None]]
    unnamed x0 -> x1, local copies, waits for them, and re-layouts: none -> 2.25 us
where the time goes in v2:
time: 80.5 us; the launch traced here: 80.3 us
  Pallas kernels  76.6 us (95%)
  local copies, waits for them, and re-layouts  2.26 us (3%)
    pallas_call x1, Pallas kernels, per_device(): pl.pallas_call(body, out_shape=jax.ShapeDtypeStruct((ROWS, D), BF16), in_...  76.6 us
    unnamed x1, local copies, waits for them, and re-layouts  2.25 us

profile of v2, /device:TPU:32, one launch (start us, length us, event | category | flops | bytes accessed | tf_op | source)
XLA Modules:
  0.0 80.3 jit_solution(4392655276703169515)
XLA Ops:
  0.7 0.1 sine_convert_fusion
  0.7 0.7 pad_maximum_fusion.emb
  1.4 76.6 %block.1 = bf16[784,640]{1,0:T(8,128)(2,1)} custom-call(bf16[784,640]{1,0:T(8,128)(2,1)} %bitcast.4, bf16[49,640]{1,0:T(8,128)(2,1)} %ref.1, bf16[1,640]{1,0:T(2,128)(2,1)} %pad_maximum_fusion.emb, f32[3,640]{1,0:T(4,128)} %gains.1, bf16[4,640,640]{2,1,0:T(8,128)(2,1)} %w_spatial.1, bf16[4,640,640]{2,1,0:T(8,128)(2,1)} %w_temporal.1, ...), custom_call_target="tpu_custom_call" | custom-call | tf_op jit(solution)/shard_map/block/pallas_call | solution.py:474
  78.0 2.2 %copy.12 = bf16[1,784,640]{2,1,0:T(8,128)(2,1)} copy(bf16[1,784,640]{2,1,0:T(8,128)(2,1)} %bitcast.3) | data formatting | bytes 2007040
  (2 shorter events, 0.0 us)

commit v3 on v2

--- a/solution.py
+++ b/solution.py
@@ -277,17 +277,18 @@
                 x[rows, c0:c1].astype(F32) + dot(attn[0:size, :], wo[:, c0:c1])
             ).astype(BF16)
 
-        @pl.loop(0, OWNERS)
-        def _(i):
-            part = pl.ds(pl.multiple_of(start + i * count, 16), count)
-            normed = norm(first[part, :].astype(F32)) * gains[1:2, :]
-            h[part, :] = (normed * (1.0 + mod[0:1, D:]) + mod[0:1, :D]).astype(BF16)
-
-        @pl.loop(1, FRAME)
+        @pl.loop(1, FRAME + 1)
         def _(d):
             @pl.when(is_owner(d))
             def _():
-                go_copy(half, d).start()
+                block = lax.min(lax.rem(me_f + d, FRAME), OWNERS - 1)
+                part = pl.ds(pl.multiple_of(start + block * count, 16), count)
+                normed = norm(first[part, :].astype(F32)) * gains[1:2, :]
+                h[part, :] = (normed * (1.0 + mod[0:1, D:]) + mod[0:1, :D]).astype(BF16)
+
+                @pl.when(d < FRAME)
+                def _():
+                    go_copy(half, d).start()
 
         @pl.when(me_f < OWNERS)
         def _():
@@ -402,18 +403,19 @@
         size = count * OWNERS
         rows = pl.ds(start, size)
 
-        @pl.loop(1, FRAME)
+        @pl.loop(0, FRAME)
         def _(d):
             @pl.when(comes_from_owner(d))
             def _():
-                back_copy(half, d).wait_recv()
-
-        @pl.loop(0, OWNERS)
-        def _(i):
-            part = pl.ds(pl.multiple_of(start + i * count, 16), count)
-            second = (first[part, :].astype(F32) + ret[part, :].astype(F32)).astype(BF16)
-            x[part, :] = second
-            first[part, :] = (norm(second.astype(F32)) * gains[2:3, :]).astype(BF16)
+                @pl.when(d > 0)
+                def _():
+                    back_copy(half, d).wait_recv()
+
+                block = lax.min(lax.rem(me_f + FRAME - d, FRAME), OWNERS - 1)
+                part = pl.ds(pl.multiple_of(start + block * count, 16), count)
+                second = (first[part, :].astype(F32) + ret[part, :].astype(F32)).astype(BF16)
+                x[part, :] = second
+                first[part, :] = (norm(second.astype(F32)) * gains[2:3, :]).astype(BF16)
 
         @pl.loop(0, 2)
         def _(i):

time: 80.5 us -> 79.9 us (level)
  no operation moved by 1% of the time
where the time goes in v3:
time: 79.9 us; the launch traced here: 79.5 us
  Pallas kernels  75.9 us (95%)
  local copies, waits for them, and re-layouts  2.26 us (3%)
    pallas_call x1, Pallas kernels, per_device(): pl.pallas_call(body, out_shape=jax.ShapeDtypeStruct((ROWS, D), BF16), in_...  75.9 us
    unnamed x1, local copies, waits for them, and re-layouts  2.25 us

profile of v3, /device:TPU:32, one launch (start us, length us, event | category | flops | bytes accessed | tf_op | source)
XLA Modules:
  0.0 79.5 jit_solution(563488952244693257)
XLA Ops:
  0.7 0.1 sine_convert_fusion
  0.7 0.7 pad_maximum_fusion.emb
  1.4 75.9 %block.1 = bf16[784,640]{1,0:T(8,128)(2,1)} custom-call(bf16[784,640]{1,0:T(8,128)(2,1)} %bitcast.4, bf16[49,640]{1,0:T(8,128)(2,1)} %ref.1, bf16[1,640]{1,0:T(2,128)(2,1)} %pad_maximum_fusion.emb, f32[3,640]{1,0:T(4,128)} %gains.1, bf16[4,640,640]{2,1,0:T(8,128)(2,1)} %w_spatial.1, bf16[4,640,640]{2,1,0:T(8,128)(2,1)} %w_temporal.1, ...), custom_call_target="tpu_custom_call" | custom-call | tf_op jit(solution)/shard_map/block/pallas_call | solution.py:476
  77.3 2.2 %copy.12 = bf16[1,784,640]{2,1,0:T(8,128)(2,1)} copy(bf16[1,784,640]{2,1,0:T(8,128)(2,1)} %bitcast.3) | data formatting | bytes 2007040
  (2 shorter events, 0.0 us)

commit v4 on v3

--- a/solution.py
+++ b/solution.py
@@ -74,11 +74,10 @@
 def body(
     lat, ref, emb, gains, w_spatial, w_temporal, w_time, w_in, w_out, out,
     x, first, h, q, k_t, v, ref_stage, ref_all, kr_t, vr, acc, held, attn, wq, wk, wv, wo,
-    ws, wt, wtime, win, wout, mod, spread, gather,
+    ws, wt, swap, wtime, win, wout, mod, spread, gather,
     recv_a, recv_b, moved_a, moved_b, ret, inner,
     sem_x, sem_w, sem_out, ref_send, ref_recv, go_send, go_recv, back_send, back_recv,
 ):
-    swap = ws.at[0]
     wtp = (ws.at[1], ws.at[2], ws.at[3], wt.at[0])
     tq, tk, tv, mixed = (w.at[0:512, 0:D] for w in (wq, wk, wv, wtime))
     result = ret
@@ -173,6 +172,16 @@
     wv[...] = jnp.zeros_like(wv)
     wo[...] = jnp.zeros_like(wo)
 
+    column = iota((D, D), 1)
+    source = HEAD * ((column & (PAD - 1)) >> 4) + 16 * (column >> 7) + (column & 15)
+    swap[...] = (iota((D, D), 0) == source).astype(F32).astype(BF16)
+    place = iota((FRAME * PAD, PAD), 0)
+    pair = FRAME * (place >> 7) + ((place & (PAD - 1)) >> 4)
+    gather[...] = ((iota((FRAME * PAD, PAD), 1) & 63) == pair).astype(F32).astype(BF16)
+    place = iota((PAD, FRAME * PAD), 1)
+    pair = FRAME * (place >> 7) + ((place & (PAD - 1)) >> 4)
+    spread[...] = (iota((PAD, FRAME * PAD), 0) == pair).astype(F32).astype(BF16)
+
     for load in loads_x:
         load.wait()
 
@@ -309,9 +318,6 @@
         )
 
     load_wt.wait()
-    column = iota((D, D), 1)
-    source = HEAD * ((column & (PAD - 1)) >> 4) + 16 * (column >> 7) + (column & 15)
-    swap[...] = (iota((D, D), 0) == source).astype(F32).astype(BF16)
     for i in range(3):
         for c0, c1 in ((0, 256), (256, 512), (512, D)):
             wtp[i][:, c0:c1] = dot(wt[i], swap[:, c0:c1]).astype(BF16)
@@ -320,13 +326,6 @@
             wtp[3][PAD * r + 16 * n : PAD * r + 16 * n + 16, :] = wt[
                 3, HEAD * n + 16 * r : HEAD * n + 16 * r + 16, :
             ]
-    place = iota((FRAME * PAD, PAD), 0)
-    pair = FRAME * (place >> 7) + ((place & (PAD - 1)) >> 4)
-    gather[...] = ((iota((FRAME * PAD, PAD), 1) & 63) == pair).astype(F32).astype(BF16)
-    place = iota((PAD, FRAME * PAD), 1)
-    pair = FRAME * (place >> 7) + ((place & (PAD - 1)) >> 4)
-    spread[...] = (iota((PAD, FRAME * PAD), 0) == pair).astype(F32).astype(BF16)
-
     @pl.when(me_f < OWNERS)
     def _():
         for half, (start, count, _) in enumerate(HALVES):
@@ -498,6 +497,7 @@
             pltpu.VMEM((WIDE, D), BF16),
             pltpu.VMEM((4, D, D), BF16),
             pltpu.VMEM((4, D, D), BF16),
+            pltpu.VMEM((D, D), BF16),
             pltpu.VMEM((D, 2 * D), BF16),
             pltpu.VMEM((D, 2 * FFH), BF16),
             pltpu.VMEM((FFH, D), BF16),

time: 79.9 us -> 79.6 us (level)
  no operation moved by 1% of the time
where the time goes in v4:
time: 79.6 us; the launch traced here: 79.2 us
  Pallas kernels  75.5 us (95%)
  local copies, waits for them, and re-layouts  2.26 us (3%)
    pallas_call x1, Pallas kernels, per_device(): pl.pallas_call(body, out_shape=jax.ShapeDtypeStruct((ROWS, D), BF16), in_...  75.5 us
    unnamed x1, local copies, waits for them, and re-layouts  2.25 us

profile of v4, /device:TPU:32, one launch (start us, length us, event | category | flops | bytes accessed | tf_op | source)
XLA Modules:
  0.0 79.2 jit_solution(6607663432000285157)
XLA Ops:
  0.7 0.1 sine_convert_fusion
  0.7 0.7 pad_maximum_fusion.emb
  1.4 75.5 %block.1 = bf16[784,640]{1,0:T(8,128)(2,1)} custom-call(bf16[784,640]{1,0:T(8,128)(2,1)} %bitcast.4, bf16[49,640]{1,0:T(8,128)(2,1)} %ref.1, bf16[1,640]{1,0:T(2,128)(2,1)} %pad_maximum_fusion.emb, f32[3,640]{1,0:T(4,128)} %gains.1, bf16[4,640,640]{2,1,0:T(8,128)(2,1)} %w_spatial.1, bf16[4,640,640]{2,1,0:T(8,128)(2,1)} %w_temporal.1, ...), custom_call_target="tpu_custom_call" | custom-call | tf_op jit(solution)/shard_map/block/pallas_call | solution.py:475
  76.9 2.2 %copy.12 = bf16[1,784,640]{2,1,0:T(8,128)(2,1)} copy(bf16[1,784,640]{2,1,0:T(8,128)(2,1)} %bitcast.3) | data formatting | bytes 2007040
  (2 shorter events, 0.0 us)
